TPU v7x, 32 devices: a whole 2x2x4 slice. The times are simulated.
32 devices in a mesh: ladder: 8 (over z, y), gx: 4 (over x, core).
Axes of the slice: x: 2, y: 2, z: 4, core: 2. Of those that a mesh axis runs over, the one named last changes fastest.
Arguments:
- field: float32 [8, 24, 96, 768], P('ladder', 'gx'), may hold values from -1.1 to 2.7
- momenta: float32 [8, 24, 96, 768], P('ladder', 'gx'), may hold values from -4 to 4
- kappas: float32 [8], replicated, may hold values from 0.1 to 0.112, as said below
- partner: int32 [8], replicated, may hold values from 0 to 7, as said below
Outputs:
- field_out: float32 [8, 24, 96, 768], P('ladder', 'gx')
- momenta_out: float32 [8, 24, 96, 768], P('ladder', 'gx')
- stats: float32 [8, 5], P('ladder')
Inputs may be any that keep to these rules, and one draw needn't show every extreme that they name: partner[partner[r]] = r; each entry is r - 1, r or r + 1; the swapping pairs all begin at indices of one parity; at least one pair swaps. kappas rise strictly along the ladder.
All inputs are finite; a program needn't handle non-finite values.
Results may differ from a plain program's by a relative error of at most 0.00002.
Values sent between devices are 32-bit elements; how exact they have to be, the bound alone decides.
A program may use at most 128 MiB of HBM per device.

v0:
```python
import jax
import jax.numpy as jnp
from jax import lax
from jax.sharding import PartitionSpec as P

NT = 8
LEAPS = 4


LAMBDA = 0.5
STEP = 0.1


def padded_2(cells, sides, width):
    for axis, dim in sides:
        count = lax.axis_size(axis)
        head = lax.slice_in_dim(cells, 0, width, axis=dim)
        tail = lax.slice_in_dim(cells, cells.shape[dim] - width, cells.shape[dim], axis=dim)
        cells = jnp.concatenate(
            [
                lax.ppermute(tail, axis, [(i, (i + 1) % count) for i in range(count)]),
                cells,
                lax.ppermute(head, axis, [((i + 1) % count, i) for i in range(count)]),
            ],
            axis=dim,
        )
    return cells


def passed_along(block, axis, distance):
    devices = range(lax.axis_size(axis))
    route = [(i - distance, i) for i in devices if i - distance in devices]
    return lax.ppermute(block, axis, route)


def carried_in(part, axis, combine, identity):
    place = lax.axis_index(axis)
    gathered = lax.all_gather(part, axis)
    state = jnp.zeros_like(part) + jnp.asarray(identity, part.dtype)

    def one(turn, state):
        return combine(state, lax.dynamic_index_in_dim(gathered, turn, 0, False))

    return lax.fori_loop(0, place, one, state)


def time_roll(arr, by):
    slot = jnp.arange(arr.shape[-1], dtype=jnp.int32) % NT
    main = jnp.roll(arr, by, -1)
    if by > 0:
        other = jnp.roll(arr, by - NT, -1)
        return jnp.where(slot == 0, other, main)
    other = jnp.roll(arr, by + NT, -1)
    return jnp.where(slot == NT - 1, other, main)


def force_of(padded, kappa):
    center = padded[1:-1]
    total = padded[2:] + padded[:-2]
    total = total + jnp.roll(center, 1, 1) + jnp.roll(center, -1, 1)
    total = total + jnp.roll(center, NT, 2) + jnp.roll(center, -NT, 2)
    total = total + time_roll(center, 1) + time_roll(center, -1)
    square = center * center
    return 2.0 * kappa * total - 2.0 * center - 4.0 * LAMBDA * (square - 1.0) * center


def local_sums(padded, moment):
    center = padded[1:-1]
    ahead = padded[2:] + jnp.roll(center, -1, 1) + jnp.roll(center, -NT, 2) + time_roll(center, -1)
    square = center * center
    hop = jnp.sum(center * ahead)
    pot = jnp.sum(square + LAMBDA * (square - 1.0) ** 2)
    kin = 0.5 * jnp.sum(moment * moment)
    return (hop, pot, kin)


def early_sums(start):
    return lax.psum((start[0], start[1], start[2]), "gx")


def widen(field):
    return padded_2(field, (("gx", 0),), 1)


def select(own, below, above, mate, rung):
    return jnp.where(mate == rung - 1, below, jnp.where(mate == rung + 1, above, own))


def per_device(field, momenta, kappas, partner):
    rung = lax.axis_index("ladder")
    count = lax.axis_size("ladder")
    mate = partner[rung]
    state = jnp.concatenate([field, momenta], 0)
    kappa = kappas[rung]
    phi = state[0]
    moment = state[1]
    padded = widen(phi)
    start = early_sums(local_sums(padded, moment))
    moment = moment + 0.5 * STEP * force_of(padded, kappa)
    for leap in range(LEAPS):
        phi = phi + STEP * moment
        padded = widen(phi)
        scale = STEP if leap < LEAPS - 1 else 0.5 * STEP
        moment = moment + scale * force_of(padded, kappa)
    finish = local_sums(padded, moment)
    finish = lax.psum((finish[0], finish[1], finish[2]), "gx")
    volume = phi.size * lax.axis_size("gx")
    energy = start[2] / volume + start[1] / volume - 2.0 * kappa * (start[0] / volume)
    values = jnp.stack([finish[0] / volume, finish[1] / volume, finish[2] / volume, energy])
    final = jnp.stack([phi, moment])
    from_below = passed_along(final, "ladder", 1)
    from_above = passed_along(final, "ladder", -1)
    final = select(final, from_below, from_above, mate, rung)
    own_kappa = kappas[rung]
    following = kappas[jnp.minimum(rung + 1, count - 1)]
    span = kappas[count - 1] - kappas[0]
    term = 2.0 * values[0] * (following - own_kappa) / span
    prior = carried_in(term, "ladder", lambda earlier, later: earlier + later, jnp.float32(0.0))
    cumulative = prior + term
    stats = jnp.concatenate([values, cumulative[None]])[None]
    return (final[0][None], final[1][None], stats)


def solution(mesh):
    in_specs = (P("ladder", "gx", None, None), P("ladder", "gx", None, None), P(), P())
    out_specs = (P("ladder", "gx", None, None), P("ladder", "gx", None, None), P("ladder", None))
    return jax.shard_map(
        per_device, mesh=mesh, in_specs=in_specs, out_specs=out_specs, check_vma=False
    )
```

profile of v0, /device:TPU:26, one launch (start us, length us, event | category | flops | bytes accessed | tf_op | source)
XLA Modules:
  0.0 274.4 jit_solution(17893536269596791886)
XLA Ops:
  0.6 2.0 slice_bitcast_fusion.1
  3.2 1.6 fusion.118
  4.8 2.0 fusion.124
  6.8 0.9 fusion.120
  7.7 1.8 fusion.125
  9.5 2.4 fusion.121
  11.9 2.4 fusion.122
  14.2 2.0 fusion.119
  16.3 0.6 fusion.126
  17.7 7.3 %multiply_add_fusion.3 = (f32[6,96,768]{2,1,0:T(8,128)S(1)}, f32[6,96,768]{2,1,0:T(8,128)S(1)}) fusion(f32[1,6,96,768]{3,2,1,0:T(8,128)S(1)} %copy-done, f32[6,96,768]{2,1,0:T(8,128)S(1)} %bitcast.40, f32[6,96,1]{2,1,0:T(8,128)} %get-tuple-element.141, f32[6,96,767]{2,1,0:T(8,128)S(1)} %get-tuple-element.143, f32[6,96,761]{2,1,0:T(8,128)} %get-tuple-element.137, ...), kind=kLoop, calls=%fused_computation.104 | loop fusion | flops 13713408 | bytes 23594500 | tf_op jit(solution)/shard_map/add | solution.py:101
  27.5 1.3 collective-permute-start.2
  29.0 6.4 %collective-permute-done.2 = f32[1,96,768]{2,1,0:T(8,128)S(1)} collective-permute-done((f32[1,96,768]{2,1,0:T(8,128)S(1)}, f32[1,96,768]{2,1,0:T(8,128)S(1)}, u32[]{:S(2)}, u32[]{:S(2)}) %collective-permute-start.2) | collective-permute-done | bytes 294944 | tf_op jit(solution)/shard_map/ppermute | solution.py:23
  35.3 2.8 %collective-permute-done.3 = f32[1,96,768]{2,1,0:T(8,128)S(1)} collective-permute-done((f32[1,96,768]{2,1,0:T(8,128)S(1)}, f32[1,96,768]{2,1,0:T(8,128)S(1)}, u32[]{:S(2)}, u32[]{:S(2)}) %collective-permute-start.3) | collective-permute-done | bytes 294944 | tf_op jit(solution)/shard_map/ppermute | solution.py:21
  38.1 3.6 %multiply_add_fusion.2 = (f32[6,96,768]{2,1,0:T(8,128)S(1)}, f32[6,96,768]{2,1,0:T(8,128)S(1)}) fusion(f32[6,96,768]{2,1,0:T(8,128)S(1)} %get-tuple-element.50, f32[6,96,768]{2,1,0:T(8,128)S(1)} %get-tuple-element.51, f32[6,96,1]{2,1,0:T(8,128)S(1)} %get-tuple-element.123, f32[6,96,767]{2,1,0:T(8,128)S(1)} %get-tuple-element.125, ...), kind=kLoop, calls=%fused_computation.103 | loop fusion | flops 13713408 | bytes 21825028 | tf_op jit(solution)/shard_map/add | solution.py:101
  44.9 5.5 %collective-permute-done.4 = f32[1,96,768]{2,1,0:T(8,128)S(1)} collective-permute-done((f32[1,96,768]{2,1,0:T(8,128)S(1)}, f32[1,96,768]{2,1,0:T(8,128)S(1)}, u32[]{:S(2)}, u32[]{:S(2)}) %collective-permute-start.4) | collective-permute-done | bytes 294944 | tf_op jit(solution)/shard_map/ppermute | solution.py:23
  50.4 3.3 %collective-permute-done.5 = f32[1,96,768]{2,1,0:T(8,128)S(1)} collective-permute-done((f32[1,96,768]{2,1,0:T(8,128)S(1)}, f32[1,96,768]{2,1,0:T(8,128)S(1)}, u32[]{:S(2)}, u32[]{:S(2)}) %collective-permute-start.5) | collective-permute-done | bytes 294944 | tf_op jit(solution)/shard_map/ppermute | solution.py:21
  53.7 3.6 %multiply_add_fusion.1 = (f32[6,96,768]{2,1,0:T(8,128)S(1)}, f32[6,96,768]{2,1,0:T(8,128)S(1)}) fusion(f32[6,96,768]{2,1,0:T(8,128)S(1)} %get-tuple-element.48, f32[6,96,768]{2,1,0:T(8,128)S(1)} %get-tuple-element.49, f32[6,96,1]{2,1,0:T(8,128)S(1)} %get-tuple-element.105, f32[6,96,767]{2,1,0:T(8,128)S(1)} %get-tuple-element.107, ...), kind=kLoop, calls=%fused_computation.102 | loop fusion | flops 13713408 | bytes 21825028 | tf_op jit(solution)/shard_map/add | solution.py:101
  60.6 5.5 %collective-permute-done.6 = f32[1,96,768]{2,1,0:T(8,128)S(1)} collective-permute-done((f32[1,96,768]{2,1,0:T(8,128)S(1)}, f32[1,96,768]{2,1,0:T(8,128)S(1)}, u32[]{:S(2)}, u32[]{:S(2)}) %collective-permute-start.6) | collective-permute-done | bytes 294944 | tf_op jit(solution)/shard_map/ppermute | solution.py:23
  66.1 2.9 %collective-permute-done.7 = f32[1,96,768]{2,1,0:T(8,128)S(1)} collective-permute-done((f32[1,96,768]{2,1,0:T(8,128)S(1)}, f32[1,96,768]{2,1,0:T(8,128)S(1)}, u32[]{:S(2)}, u32[]{:S(2)}) %collective-permute-start.7) | collective-permute-done | bytes 294944 | tf_op jit(solution)/shard_map/ppermute | solution.py:21
  69.0 3.6 %multiply_add_fusion = (f32[6,96,768]{2,1,0:T(8,128)S(1)}, f32[6,96,768]{2,1,0:T(8,128)S(1)}) fusion(f32[6,96,768]{2,1,0:T(8,128)S(1)} %get-tuple-element.46, f32[6,96,768]{2,1,0:T(8,128)S(1)} %get-tuple-element.47, f32[6,96,1]{2,1,0:T(8,128)S(1)} %get-tuple-element.87, f32[6,96,767]{2,1,0:T(8,128)S(1)} %get-tuple-element.89, ...), kind=kLoop, calls=%fused_computation.101 | loop fusion | flops 13713408 | bytes 21825028 | tf_op jit(solution)/shard_map/add | solution.py:101
  73.0 0.6 fusion.86
  73.6 0.6 fusion.87
  74.6 0.6 fusion.90
  75.9 5.5 %collective-permute-done.8 = f32[1,96,768]{2,1,0:T(8,128)S(1)} collective-permute-done((f32[1,96,768]{2,1,0:T(8,128)S(1)}, f32[1,96,768]{2,1,0:T(8,128)S(1)}, u32[]{:S(2)}, u32[]{:S(2)}) %collective-permute-start.8) | collective-permute-done | bytes 294944 | tf_op jit(solution)/shard_map/ppermute | solution.py:23
  81.5 2.9 %collective-permute-done.9 = f32[1,96,768]{2,1,0:T(8,128)S(1)} collective-permute-done((f32[1,96,768]{2,1,0:T(8,128)S(1)}, f32[1,96,768]{2,1,0:T(8,128)S(1)}, u32[]{:S(2)}, u32[]{:S(2)}) %collective-permute-start.9) | collective-permute-done | bytes 294944 | tf_op jit(solution)/shard_map/ppermute | solution.py:21
  84.4 4.1 %multiply_reduce_fusion = (f32[]{:T(128)}, f32[6,96,768]{2,1,0:T(8,128)S(1)}) fusion(f32[6,96,768]{2,1,0:T(8,128)S(1)} %get-tuple-element.45, f32[6,96,768]{2,1,0:T(8,128)S(1)} %get-tuple-element.44, f32[6,96,1]{2,1,0:T(8,128)S(1)} %get-tuple-element.69, f32[6,96,767]{2,1,0:T(8,128)S(1)} %get-tuple-element.71, f32[6,96,761]{2,1,0:T(8,128)S(1)} %get-tuple-element.65, ...), kind=kLoop, calls=%fused_computation.99 | loop fusion | flops 13713407 | bytes 20055560 | tf_op jit(solution)/shard_map/reduce_sum | solution.py:73
  88.5 2.3 pad_maximum_fusion
  90.9 3.3 %collective-permute-start.11 = (f32[2,6,96,768]{3,2,1,0:T(8,128)}, f32[2,6,96,768]{3,2,1,0:T(8,128)}, u32[]{:S(2)}, u32[]{:S(2)}) collective-permute-start(f32[2,6,96,768]{3,2,1,0:T(8,128)} %pad_maximum_fusion), channel_id=1, source_target_pairs={{4,0},{8,4},{12,8},{16,12},{20,16},{24,20},{28,24},{5,1},{9,5},{13... | collective-permute-start | bytes 10616840 | tf_op jit(solution)/shard_map/ppermute | solution.py:33
  94.2 4.4 %collective-permute-start.10 = (f32[2,6,96,768]{3,2,1,0:T(8,128)}, f32[2,6,96,768]{3,2,1,0:T(8,128)}, u32[]{:S(2)}, u32[]{:S(2)}) collective-permute-start(f32[2,6,96,768]{3,2,1,0:T(8,128)} %pad_maximum_fusion), channel_id=1, source_target_pairs={{0,4},{4,8},{8,12},{12,16},{16,20},{20,24},{24,28},{1,5},{5,9},{9,... | collective-permute-start | bytes 10616840 | tf_op jit(solution)/shard_map/ppermute | solution.py:33
  98.6 0.7 dynamic_slice.14
  101.2 2.5 fusion.70
  104.3 1.1 add_reduce_fusion
  106.0 0.6 dynamic-slice
  107.8 4.8 %fusion.69 = f32[]{:T(128)} fusion(f32[6,96,768]{2,1,0:T(8,128)S(1)} %bitcast.41, f32[1,96,768]{2,1,0:T(8,128)} %collective-permute-done, f32[6,1,768]{2,1,0:T(1,128)} %get-tuple-element.129, f32[6,95,768]{2,1,0:T(8,128)} %get-tuple-element.131, f32[6,96,8]{2,1,0:T(8,128)} %get-tuple-element.133, f32[6,96,760]{2,1,0:T(8,128)} %get-tuple-element.135, ...), kind=kLoop, calls=%fused_computation.81 | loop fusion | flops 4866047 | bytes 9143044 | tf_op jit(solution)/shard_map/reduce_sum | solution.py:71
  113.2 4.9 %add_reduce_fusion.1 = (f32[]{:T(128)}, f32[]{:T(128)}) fusion(f32[6,96,768]{2,1,0:T(8,128)S(1)} %get-tuple-element.44, f32[6,96,1]{2,1,0:T(8,128)} %copy-done.9, f32[6,96,767]{2,1,0:T(8,128)} %copy-done.7, f32[6,96,761]{2,1,0:T(8,128)} %copy-done.5, f32[6,96,7]{2,1,0:T(8,128)} %copy-done.11, pred[768]{0:T(1024)(128)(4,1)S(1)} %get-tuple-element.148, ...), kind=kLoop, calls=%fused_computation.100 | loop fusion | flops 7520254 | bytes 9143048 | tf_op jit(solution)/shard_map/reduce_sum | solution.py:72
  118.1 6.7 %all-reduce.1 = (f32[]{:T(128)}, f32[]{:T(128)}, f32[]{:T(128)}, f32[]{:T(128)}, f32[]{:T(128)}) all-reduce(f32[]{:T(128)} %get-tuple-element.28, f32[]{:T(128)} %get-tuple-element.27, f32[]{:T(128)S(6)} %mul.193, f32[]{:T(128)S(6)} %add.306, f32[]{:T(128)} %fusion.69), channel_id=1, replica_groups=mesh['ladder'=8,'gx'=4] {'gx'}, use_global_device_ids=true, to_apply=%region_1.2 | all-reduce | flops 5 | bytes 40 | tf_op jit(solution)/shard_map/psum | solution.py:106
  125.6 0.7 dynamic-update-slice
  126.9 130.8 %all-reduce = f32[8]{0:T(128)S(1)} all-reduce(f32[8]{0:T(128)S(1)} %dynamic-update-slice), channel_id=1, replica_groups=mesh['ladder'=8,'gx'=4] {'ladder'}, use_global_device_ids=true, to_apply=%add | all-reduce | flops 8 | bytes 64
  261.4 7.6 %while.10 = (s32[]{:T(128)}, f32[]{:T(128)}, s32[]{:T(128)}, f32[8]{0:T(128)S(1)}, s32[]{:T(128)}, /*index=5*/s32[]{:T(128)}, s32[]{:T(128)}) while((s32[]{:T(128)}, f32[]{:T(128)}, s32[]{:T(128)}, f32[8]{0:T(128)S(1)}, s32[]{:T(128)}, /*index=5*/s32[]{:T(128)}, s32[]{:T(128)}) %tuple.78), condition=%wide.region_13.14_spmd, body=%wide.region_12.13_spmd.sunk | while | flops 6 | bytes 143 | solution.py:44
  261.4 0.6 dynamic_slice.20
  262.7 0.6 dynamic_slice.20
  264.0 0.6 dynamic_slice.20
  265.2 0.6 dynamic_slice.20
  266.5 0.6 dynamic_slice.20
  267.8 0.6 dynamic_slice.20
  269.1 0.6 concatenate.224
  269.7 2.7 select_select_fusion
  272.3 2.0 fusion.81
  (83 shorter events, 11.0 us)
Async XLA Ops:
  0.6 6.1 %copy-start = (f32[1,6,96,768]{3,2,1,0:T(8,128)S(1)}, f32[1,6,96,768]{3,2,1,0:T(8,128)}, u32[]{:S(2)}) copy-start(f32[1,6,96,768]{3,2,1,0:T(8,128)} %param.6) | copy-start | bytes 5308420
  2.7 15.0 %collective-permute-start = (f32[1,96,768]{2,1,0:T(8,128)}, f32[1,96,768]{2,1,0:T(8,128)}, u32[]{:S(2)}, u32[]{:S(2)}) collective-permute-start(f32[1,96,768]{2,1,0:T(8,128)} %get-tuple-element.126), channel_id=1, source_target_pairs={{1,0},{2,1},{3,2},{0,3},{5,4},{6,5},{7,6},{4,7},{9,8},{10,9},{11,1... | collective-permute-start | bytes 884744 | tf_op jit(solution)/shard_map/ppermute | solution.py:23
  2.7 15.0 %collective-permute-start.1 = (f32[1,96,768]{2,1,0:T(8,128)}, f32[1,96,768]{2,1,0:T(8,128)}, u32[]{:S(2)}, u32[]{:S(2)}) collective-permute-start(f32[1,96,768]{2,1,0:T(8,128)} %get-tuple-element.127), channel_id=1, source_target_pairs={{0,1},{1,2},{2,3},{3,0},{4,5},{5,6},{6,7},{7,4},{8,9},{9,10},{10,1... | collective-permute-start | bytes 884744 | tf_op jit(solution)/shard_map/ppermute | solution.py:21
  9.5 8.2 %copy-start.3 = (f32[6,96,767]{2,1,0:T(8,128)}, f32[6,96,767]{2,1,0:T(8,128)S(1)}, u32[]{:S(2)}) copy-start(f32[6,96,767]{2,1,0:T(8,128)S(1)} %get-tuple-element.143) | copy-start | bytes 5301508
  14.2 2.0 copy-start.14
  17.7 7.4 %copy-start.8 = (f32[6,96,7]{2,1,0:T(8,128)}, f32[6,96,7]{2,1,0:T(8,128)S(1)}, u32[]{:S(2)}) copy-start(f32[6,96,7]{2,1,0:T(8,128)S(1)} %get-tuple-element.139) | copy-start | bytes 48388
  27.5 7.8 %collective-permute-start.2 = (f32[1,96,768]{2,1,0:T(8,128)S(1)}, f32[1,96,768]{2,1,0:T(8,128)S(1)}, u32[]{:S(2)}, u32[]{:S(2)}) collective-permute-start(f32[1,96,768]{2,1,0:T(8,128)S(1)} %get-tuple-element.108), channel_id=1, source_target_pairs={{1,0},{2,1},{3,2},{0,3},{5,4},{6,5},{7,6},{4,7},{9,8},{10,9},{11,1... | collective-permute-start | bytes 884744 | tf_op jit(solution)/shard_map/ppermute | solution.py:23
  28.8 9.3 %collective-permute-start.3 = (f32[1,96,768]{2,1,0:T(8,128)S(1)}, f32[1,96,768]{2,1,0:T(8,128)S(1)}, u32[]{:S(2)}, u32[]{:S(2)}) collective-permute-start(f32[1,96,768]{2,1,0:T(8,128)S(1)} %get-tuple-element.109), channel_id=1, source_target_pairs={{0,1},{1,2},{2,3},{3,0},{4,5},{5,6},{6,7},{7,4},{8,9},{9,10},{10,1... | collective-permute-start | bytes 884744 | tf_op jit(solution)/shard_map/ppermute | solution.py:21
  44.2 6.3 %collective-permute-start.4 = (f32[1,96,768]{2,1,0:T(8,128)S(1)}, f32[1,96,768]{2,1,0:T(8,128)S(1)}, u32[]{:S(2)}, u32[]{:S(2)}) collective-permute-start(f32[1,96,768]{2,1,0:T(8,128)S(1)} %get-tuple-element.90), channel_id=1, source_target_pairs={{1,0},{2,1},{3,2},{0,3},{5,4},{6,5},{7,6},{4,7},{9,8},{10,9},{11,1... | collective-permute-start | bytes 884744 | tf_op jit(solution)/shard_map/ppermute | solution.py:23
  44.2 9.5 %collective-permute-start.5 = (f32[1,96,768]{2,1,0:T(8,128)S(1)}, f32[1,96,768]{2,1,0:T(8,128)S(1)}, u32[]{:S(2)}, u32[]{:S(2)}) collective-permute-start(f32[1,96,768]{2,1,0:T(8,128)S(1)} %get-tuple-element.91), channel_id=1, source_target_pairs={{0,1},{1,2},{2,3},{3,0},{4,5},{5,6},{6,7},{7,4},{8,9},{9,10},{10,1... | collective-permute-start | bytes 884744 | tf_op jit(solution)/shard_map/ppermute | solution.py:21
  59.8 6.3 %collective-permute-start.6 = (f32[1,96,768]{2,1,0:T(8,128)S(1)}, f32[1,96,768]{2,1,0:T(8,128)S(1)}, u32[]{:S(2)}, u32[]{:S(2)}) collective-permute-start(f32[1,96,768]{2,1,0:T(8,128)S(1)} %get-tuple-element.72), channel_id=1, source_target_pairs={{1,0},{2,1},{3,2},{0,3},{5,4},{6,5},{7,6},{4,7},{9,8},{10,9},{11,1... | collective-permute-start | bytes 884744 | tf_op jit(solution)/shard_map/ppermute | solution.py:23
  59.9 9.1 %collective-permute-start.7 = (f32[1,96,768]{2,1,0:T(8,128)S(1)}, f32[1,96,768]{2,1,0:T(8,128)S(1)}, u32[]{:S(2)}, u32[]{:S(2)}) collective-permute-start(f32[1,96,768]{2,1,0:T(8,128)S(1)} %get-tuple-element.73), channel_id=1, source_target_pairs={{0,1},{1,2},{2,3},{3,0},{4,5},{5,6},{6,7},{7,4},{8,9},{9,10},{10,1... | collective-permute-start | bytes 884744 | tf_op jit(solution)/shard_map/ppermute | solution.py:21
  72.8 11.6 %copy-start.9 = (f32[6,96,1]{2,1,0:T(8,128)}, f32[6,96,1]{2,1,0:T(8,128)S(1)}, u32[]{:S(2)}) copy-start(f32[6,96,1]{2,1,0:T(8,128)S(1)} %get-tuple-element.69) | copy-start | bytes 6916
  73.0 11.4 %copy-start.10 = (f32[6,96,8]{2,1,0:T(8,128)}, f32[6,96,8]{2,1,0:T(8,128)S(1)}, u32[]{:S(2)}) copy-start(f32[6,96,8]{2,1,0:T(8,128)S(1)} %get-tuple-element.61) | copy-start | bytes 55300
  73.6 10.8 %copy-start.4 = (f32[6,96,760]{2,1,0:T(8,128)}, f32[6,96,760]{2,1,0:T(8,128)S(1)}, u32[]{:S(2)}) copy-start(f32[6,96,760]{2,1,0:T(8,128)S(1)} %get-tuple-element.63) | copy-start | bytes 5253124
  74.2 10.1 %copy-start.5 = (f32[6,96,761]{2,1,0:T(8,128)}, f32[6,96,761]{2,1,0:T(8,128)S(1)}, u32[]{:S(2)}) copy-start(f32[6,96,761]{2,1,0:T(8,128)S(1)} %get-tuple-element.65) | copy-start | bytes 5260036
  74.6 9.8 %copy-start.6 = (f32[6,95,768]{2,1,0:T(8,128)}, f32[6,95,768]{2,1,0:T(8,128)S(1)}, u32[]{:S(2)}) copy-start(f32[6,95,768]{2,1,0:T(8,128)S(1)} %get-tuple-element.59) | copy-start | bytes 5253124
  75.2 13.3 %copy-start.7 = (f32[6,96,767]{2,1,0:T(8,128)}, f32[6,96,767]{2,1,0:T(8,128)S(1)}, u32[]{:S(2)}) copy-start(f32[6,96,767]{2,1,0:T(8,128)S(1)} %get-tuple-element.71) | copy-start | bytes 5301508
  75.2 6.3 %collective-permute-start.8 = (f32[1,96,768]{2,1,0:T(8,128)S(1)}, f32[1,96,768]{2,1,0:T(8,128)S(1)}, u32[]{:S(2)}, u32[]{:S(2)}) collective-permute-start(f32[1,96,768]{2,1,0:T(8,128)S(1)} %get-tuple-element.54), channel_id=1, source_target_pairs={{1,0},{2,1},{3,2},{0,3},{5,4},{6,5},{7,6},{4,7},{9,8},{10,9},{11,1... | collective-permute-start | bytes 884744 | tf_op jit(solution)/shard_map/ppermute | solution.py:23
  75.3 9.1 %collective-permute-start.9 = (f32[1,96,768]{2,1,0:T(8,128)S(1)}, f32[1,96,768]{2,1,0:T(8,128)S(1)}, u32[]{:S(2)}, u32[]{:S(2)}) collective-permute-start(f32[1,96,768]{2,1,0:T(8,128)S(1)} %get-tuple-element.55), channel_id=1, source_target_pairs={{0,1},{1,2},{2,3},{3,0},{4,5},{5,6},{6,7},{7,4},{8,9},{9,10},{10,1... | collective-permute-start | bytes 884744 | tf_op jit(solution)/shard_map/ppermute | solution.py:21
  75.8 12.7 %copy-start.13 = (f32[6,1,768]{2,1,0:T(1,128)}, f32[6,1,768]{2,1,0:T(1,128)S(1)}, u32[]{:S(2)}) copy-start(f32[6,1,768]{2,1,0:T(1,128)S(1)} %get-tuple-element.57) | copy-start | bytes 55300
  75.9 12.6 %copy-start.11 = (f32[6,96,7]{2,1,0:T(8,128)}, f32[6,96,7]{2,1,0:T(8,128)S(1)}, u32[]{:S(2)}) copy-start(f32[6,96,7]{2,1,0:T(8,128)S(1)} %get-tuple-element.67) | copy-start | bytes 48388
  81.5 7.1 %copy-start.12 = (f32[1,96,768]{2,1,0:T(8,128)}, f32[1,96,768]{2,1,0:T(8,128)S(1)}, u32[]{:S(2)}) copy-start(f32[1,96,768]{2,1,0:T(8,128)S(1)} %collective-permute-done.8) | copy-start | bytes 884740
  88.5 2.4 copy-start.1
  88.5 10.1 %copy-start.15 = (s32[8]{0:T(128)S(1)}, s32[8]{0:T(128)}, u32[]{:S(2)}) copy-start(s32[8]{0:T(128)} %param.9) | copy-start | bytes 100
  90.9 178.8 %collective-permute-start.11 = (f32[2,6,96,768]{3,2,1,0:T(8,128)}, f32[2,6,96,768]{3,2,1,0:T(8,128)}, u32[]{:S(2)}, u32[]{:S(2)}) collective-permute-start(f32[2,6,96,768]{3,2,1,0:T(8,128)} %pad_maximum_fusion), channel_id=1, source_target_pairs={{4,0},{8,4},{12,8},{16,12},{20,16},{24,20},{28,24},{5,1},{9,5},{13... | collective-permute-start | bytes 10616840 | tf_op jit(solution)/shard_map/ppermute | solution.py:33
  94.2 175.5 %collective-permute-start.10 = (f32[2,6,96,768]{3,2,1,0:T(8,128)}, f32[2,6,96,768]{3,2,1,0:T(8,128)}, u32[]{:S(2)}, u32[]{:S(2)}) collective-permute-start(f32[2,6,96,768]{3,2,1,0:T(8,128)} %pad_maximum_fusion), channel_id=1, source_target_pairs={{0,4},{4,8},{8,12},{12,16},{16,20},{20,24},{24,28},{1,5},{5,9},{9,... | collective-permute-start | bytes 10616840 | tf_op jit(solution)/shard_map/ppermute | solution.py:33
  101.2 4.8 %copy-start.16 = (u32[32]{0:T(128)S(1)}, u32[32]{0:T(128)}, u32[]{:S(2)}) copy-start(u32[32]{0:T(128)} %constant.105) | copy-start | bytes 388
  113.2 156.5 %copy-start.2 = (f32[6,96,768]{2,1,0:T(8,128)S(1)}, f32[6,96,768]{2,1,0:T(8,128)}, u32[]{:S(2)}) copy-start(f32[6,96,768]{2,1,0:T(8,128)} %copy-done.1) | copy-start | bytes 5308420
where the time goes:
time: 275 us; the launch traced here: 274 us
  blocking collectives  138 us (50%)
  other arithmetic  40.6 us (15%)
  waiting for transfers between devices  34.8 us (13%)
  local copies, waits for them, and re-layouts  34.6 us (13%)
  between operations  11.7 us (4%)
  starting transfers between devices  11.2 us (4%)
  loops' own time  3.97 us (1%)
    unnamed x1, blocking collectives  131 us
    ppermute x5, waiting for transfers between devices, padded_2(): lax.ppermute(head, axis, [((i + 1) % count, i) for i in range(count)])  22.9 us
    add x4, other arithmetic, per_device(): phi = phi + STEP * moment  18.2 us
    ppermute x5, waiting for transfers between devices, padded_2(): lax.ppermute(tail, axis, [(i, (i + 1) % count) for i in range(count)])  11.9 us
    ppermute x2, starting transfers between devices, passed_along(): return lax.ppermute(block, axis, route)  7.7 us
    psum x1, blocking collectives, per_device(): finish = lax.psum((finish[0], finish[1], finish[2]), 'gx')  6.74 us
    slice x10, local copies, waits for them, and re-layouts, time_roll(): main = jnp.roll(arr, by, -1)  6.7 us
    reduce_sum x2, other arithmetic, local_sums(): kin = 0.5 * jnp.sum(moment * moment)  6.64 us
  transfers between devices with their start and end apart: 12, of which 8 were waited for; matrix products, arithmetic and copies ran while one was open for 12% of the time, Pallas kernels for 0%

commit v1 on v0

v1 whole, which is shorter than its diff:
```python
import functools

import jax
import jax.numpy as jnp
from jax import lax
from jax.experimental import pallas as pl
from jax.experimental.pallas import tpu as pltpu
from jax.sharding import PartitionSpec as P

NT = 8
LEAPS = 4
LAMBDA = 0.5
STEP = 0.1

ROWS = 16
LAG = 2
STAGES = LEAPS + 1
LANES = 128
MESH = pl.DeviceIdType.MESH


def shifted_t(tile, slot):
    ahead = jnp.where(slot == NT - 1, pltpu.roll(tile, NT - 1, 1), pltpu.roll(tile, LANES - 1, 1))
    behind = jnp.where(slot == 0, pltpu.roll(tile, LANES - NT + 1, 1), pltpu.roll(tile, 1, 1))
    return ahead + behind


def zt_sum(cur, lane, slot):
    count = cur.shape[1] // LANES
    tiles = [cur[:, k * LANES : (k + 1) * LANES] for k in range(count)]
    up = [pltpu.roll(t, NT, 1) for t in tiles]
    down = [pltpu.roll(t, LANES - NT, 1) for t in tiles]
    sums = []
    for k in range(count):
        below = jnp.where(lane < NT, up[k - 1], up[k])
        above = jnp.where(lane >= LANES - NT, down[(k + 1) % count], down[k])
        sums.append(below + above + shifted_t(tiles[k], slot))
    return jnp.concatenate(sums, axis=1)


def fold(block):
    total = block[:, :LANES]
    for k in range(1, block.shape[1] // LANES):
        total = total + block[:, k * LANES : (k + 1) * LANES]
    return total


def body(
    odd, ring, rungs, kappas, partner, field, momenta,
    field_out, momenta_out, stats,
    fb, pb, halo, got_f, got_p, acc, own, gx_buf, rung_buf,
    load_sem, halo_send, halo_recv, swap_send, swap_recv, out_sem,
    gx_send, gx_recv, rung_send, rung_recv,
):
    planes, height, width = pb.shape
    chunks = height // ROWS
    rung = lax.axis_index("ladder")
    me = lax.axis_index("gx")
    right = lax.rem(me + 1, ring)
    left = lax.rem(me + ring - 1, ring)
    even_place = lax.rem(rung, 2) == 0
    if odd:
        paired = (rung > 0) & (rung < rungs - 1)
        mate = jnp.where(even_place, rung - 1, rung + 1)
        mate = jnp.where(paired, mate, rung)
    else:
        paired = None
        mate = jnp.where(even_place, rung + 1, rung - 1)

    def when_paired(todo):
        if odd:
            pl.when(paired)(todo)
        else:
            todo()

    loads = [
        pltpu.make_async_copy(field.at[0], fb.at[0], load_sem.at[0]),
        pltpu.make_async_copy(momenta.at[0], pb, load_sem.at[1]),
    ]
    for load in loads:
        load.start()

    barrier = pltpu.get_barrier_semaphore()
    for off in range(1, ring):
        pl.semaphore_signal(barrier, inc=1, device_id=(rung, lax.rem(me + off, ring)), device_id_type=MESH)
    for off in range(1, rungs):
        pl.semaphore_signal(barrier, inc=1, device_id=(lax.rem(rung + off, rungs), me), device_id_type=MESH)
    pl.semaphore_wait(barrier, ring - 1 + rungs - 1)

    def span(c):
        return pl.ds(pl.multiple_of(c * ROWS, ROWS), ROWS)

    def halo_copies(stage, c):
        rows = span(c)
        if stage == 0:
            low, high = field.at[0, 0, rows], field.at[0, planes - 1, rows]
        else:
            low, high = fb.at[stage, 0, rows], fb.at[stage, planes - 1, rows]
        down = pltpu.make_async_remote_copy(
            src_ref=low, dst_ref=halo.at[stage, 1, rows],
            send_sem=halo_send.at[stage, 1, c], recv_sem=halo_recv.at[stage, 1, c],
            device_id=(rung, left), device_id_type=MESH,
        )
        up = pltpu.make_async_remote_copy(
            src_ref=high, dst_ref=halo.at[stage, 0, rows],
            send_sem=halo_send.at[stage, 0, c], recv_sem=halo_recv.at[stage, 0, c],
            device_id=(rung, right), device_id_type=MESH,
        )
        return down, up

    def swap_copy(which, c):
        rows = span(c)
        src = fb.at[LEAPS, :, rows] if which == 0 else pb.at[:, rows]
        dst = got_f if which == 0 else got_p
        return pltpu.make_async_remote_copy(
            src_ref=src, dst_ref=dst.at[:, rows],
            send_sem=swap_send.at[which, c], recv_sem=swap_recv.at[which, c],
            device_id=(mate, me), device_id_type=MESH,
        )

    def first_halo(c, carry):
        for copy in halo_copies(0, c):
            copy.start()
        return carry

    lax.fori_loop(0, chunks, first_halo, 0)

    acc[...] = jnp.zeros_like(acc)
    kappa = kappas[rung]
    lane = lax.broadcasted_iota(jnp.int32, (8, LANES), 1)
    slot = lane % NT
    row = lax.broadcasted_iota(jnp.int32, (8, width), 0)

    for load in loads:
        load.wait()

    def unit(stage, c):
        for copy in halo_copies(stage, c):
            copy.wait_recv()
        scale = STEP if 0 < stage < LEAPS else 0.5 * STEP
        of_sum = (2.0 * scale) * kappa

        def group(g, carry):
            base = c * ROWS + g * 8
            at = pl.ds(pl.multiple_of(base, 8), 8)
            before = pl.ds(pl.multiple_of(lax.rem(base + height - 8, height), 8), 8)
            after = pl.ds(pl.multiple_of(lax.rem(base + 8, height), 8), 8)
            hop = pot = kin = None
            for x in range(planes):
                cur = fb[stage, x, at, :]
                below = fb[stage, x - 1, at, :] if x > 0 else halo[stage, 0, at, :]
                above = fb[stage, x + 1, at, :] if x < planes - 1 else halo[stage, 1, at, :]
                up = pltpu.roll(jnp.where(row == 7, fb[stage, x, before, :], cur), 1, 0)
                down = pltpu.roll(jnp.where(row == 0, fb[stage, x, after, :], cur), 7, 0)
                total = (below + above) + (up + down) + zt_sum(cur, lane, slot)
                square = cur * cur
                moment = pb[x, at, :]
                fresh = moment + of_sum * total - (2.0 * scale) * (square * cur)
                pb[x, at, :] = fresh
                if stage < LEAPS:
                    fb[stage + 1, x, at, :] = cur + STEP * fresh
                if stage == 0 or stage == LEAPS:
                    kept = moment if stage == 0 else fresh
                    parts = (fold(cur * total), fold(square * square), fold(kept * kept))
                    if hop is None:
                        hop, pot, kin = parts
                    else:
                        hop, pot, kin = hop + parts[0], pot + parts[1], kin + parts[2]
            if stage == 0 or stage == LEAPS:
                first = 0 if stage == 0 else 3
                acc[first] += hop
                acc[first + 1] += pot
                acc[first + 2] += kin
            return carry

        lax.fori_loop(0, ROWS // 8, group, 0)
        if stage < LEAPS:
            for copy in halo_copies(stage + 1, c):
                copy.start()
        if stage >= LEAPS - 1:
            when_paired(lambda: swap_copy(stage - LEAPS + 1, c).start())

    def iteration(i, carry):
        for stage in range(STAGES):
            k = i - LAG * stage

            @pl.when((k >= 0) & (k < chunks))
            def _(stage=stage, k=k):
                unit(stage, lax.rem(stage + k, chunks))

        return carry

    lax.fori_loop(0, chunks + LAG * LEAPS, iteration, 0)

    volume = float(planes * ring * height * width)
    for j in range(6):
        part = jnp.sum(jnp.sum(acc[j], axis=0, keepdims=True), axis=1, keepdims=True)
        own[j : j + 1, :] = jnp.broadcast_to(part, (1, LANES))
    own[6:8, :] = jnp.zeros((2, LANES), jnp.float32)
    gx_buf[me] = own[...]

    def gx_copy(source, target):
        return pltpu.make_async_remote_copy(
            src_ref=own, dst_ref=gx_buf.at[source],
            send_sem=gx_send.at[target], recv_sem=gx_recv.at[source],
            device_id=(rung, target), device_id_type=MESH,
        )

    for off in range(1, ring):
        gx_copy(me, lax.rem(me + off, ring)).start()
    for off in range(1, ring):
        there = lax.rem(me + off, ring)
        gx_copy(there, there).wait_recv()
    total = gx_buf[0]
    for i in range(1, ring):
        total = total + gx_buf[i]
    rung_buf[rung] = total

    def rung_copy(source, target):
        return pltpu.make_async_remote_copy(
            src_ref=rung_buf.at[rung], dst_ref=rung_buf.at[source],
            send_sem=rung_send.at[target], recv_sem=rung_recv.at[source],
            device_id=(target, me), device_id_type=MESH,
        )

    for off in range(1, rungs):
        rung_copy(rung, lax.rem(rung + off, rungs)).start()

    swaps = partner[rung] != rung

    def out_copy(which, c, source):
        rows = span(c)
        dst = field_out if which == 0 else momenta_out
        return pltpu.make_async_copy(source.at[:, rows], dst.at[0, :, rows], out_sem.at[which, c])

    def settle(which, c):
        got = got_f if which == 0 else got_p
        rows = span(c)

        def arrived():
            swap_copy(which, c).wait_recv()
            mine = fb[LEAPS, :, rows, :] if which == 0 else pb[:, rows, :]
            got[:, rows, :] = jnp.where(swaps, got[:, rows, :], mine)

        def alone():
            got[:, rows, :] = fb[LEAPS, :, rows, :] if which == 0 else pb[:, rows, :]

        if odd:
            pl.when(paired)(arrived)
            pl.when(jnp.logical_not(paired))(alone)
        else:
            arrived()
        out_copy(which, c, got).start()

    def finish(k, carry):
        for which in range(2):
            settle(which, lax.rem(LEAPS - 1 + which + k, chunks))
        return carry

    lax.fori_loop(0, chunks, finish, 0)

    for off in range(1, rungs):
        there = lax.rem(rung + off, rungs)
        rung_copy(there, there).wait_recv()
    width_of = jnp.full((1, LANES), kappas[rungs - 1] - kappas[0], jnp.float32)
    cumulative = jnp.zeros((1, LANES), jnp.float32)
    for j in range(rungs - 1):
        gap = kappas[j + 1] - kappas[j]
        term = 2.0 * (rung_buf[j][3:4, :] * (0.5 / volume)) * gap / width_of
        cumulative = cumulative + jnp.where(rung >= j, term, jnp.zeros_like(term))
    mean = total * (1.0 / volume)
    energy = 0.5 * mean[2:3, :] + (0.5 * mean[1:2, :] + 0.5) - kappa * mean[0:1, :]
    spot = lax.broadcasted_iota(jnp.int32, (1, LANES), 1)
    line = jnp.where(spot == 0, 0.5 * mean[3:4, :], 0.5 * mean[4:5, :] + 0.5)
    line = jnp.where(spot == 2, 0.5 * mean[5:6, :], line)
    line = jnp.where(spot == 3, energy, line)
    line = jnp.where(spot == 4, cumulative, line)
    stats[...] = line[:, 0:5]

    def close(c, carry):
        for stage in range(STAGES):
            for copy in halo_copies(stage, c):
                copy.wait_send()
        for which in range(2):
            when_paired(lambda which=which: swap_copy(which, c).wait_send())
            out_copy(which, c, got_f if which == 0 else got_p).wait()
        return carry

    lax.fori_loop(0, chunks, close, 0)
    for off in range(1, ring):
        gx_copy(me, lax.rem(me + off, ring)).wait_send()
    for off in range(1, rungs):
        rung_copy(rung, lax.rem(rung + off, rungs)).wait_send()


def step(odd, kappas, partner, field, momenta):
    ring, rungs = lax.axis_size("gx"), lax.axis_size("ladder")
    _, planes, height, width = field.shape
    chunks = height // ROWS
    f32 = jnp.float32
    slab = (planes, height, width)
    dma = pltpu.SemaphoreType.DMA
    sites = planes * height * width
    return pl.pallas_call(
        functools.partial(body, odd, ring, rungs),
        out_shape=[
            jax.ShapeDtypeStruct(field.shape, f32),
            jax.ShapeDtypeStruct(field.shape, f32),
            jax.ShapeDtypeStruct((1, 5), f32),
        ],
        in_specs=[pl.BlockSpec(memory_space=pltpu.SMEM)] * 2 + [pl.BlockSpec(memory_space=pl.ANY)] * 2,
        out_specs=[pl.BlockSpec(memory_space=pl.ANY)] * 2 + [pl.BlockSpec(memory_space=pltpu.VMEM)],
        scratch_shapes=[
            pltpu.VMEM((STAGES,) + slab, f32),
            pltpu.VMEM(slab, f32),
            pltpu.VMEM((STAGES, 2, height, width), f32),
            pltpu.VMEM(slab, f32),
            pltpu.VMEM(slab, f32),
            pltpu.VMEM((6, 8, LANES), f32),
            pltpu.VMEM((8, LANES), f32),
            pltpu.VMEM((ring, 8, LANES), f32),
            pltpu.VMEM((rungs, 8, LANES), f32),
            dma((2,)),
            dma((STAGES, 2, chunks)),
            dma((STAGES, 2, chunks)),
            dma((2, chunks)),
            dma((2, chunks)),
            dma((2, chunks)),
            dma((ring,)),
            dma((ring,)),
            dma((rungs,)),
            dma((rungs,)),
        ],
        compiler_params=pltpu.CompilerParams(
            collective_id=odd, has_side_effects=True, vmem_limit_bytes=48 * 2**20
        ),
        cost_estimate=pl.CostEstimate(flops=150 * sites, bytes_accessed=16 * sites, transcendentals=0),
        name="odd_pairs" if odd else "even_pairs",
    )(kappas, partner, field, momenta)


def per_device(field, momenta, kappas, partner):
    place = jnp.arange(partner.shape[0], dtype=jnp.int32)
    odd = jnp.any((partner == place + 1) & (place % 2 == 1))
    return tuple(
        lax.cond(
            odd, functools.partial(step, 1), functools.partial(step, 0), kappas, partner, field, momenta
        )
    )


def solution(mesh):
    in_specs = (P("ladder", "gx", None, None), P("ladder", "gx", None, None), P(), P())
    out_specs = (P("ladder", "gx", None, None), P("ladder", "gx", None, None), P("ladder", None))
    return jax.shard_map(
        per_device, mesh=mesh, in_specs=in_specs, out_specs=out_specs, check_vma=False
    )
```

time: 275 us -> 115 us (0.42)
  the two profiles are of different devices: /device:TPU:26 before, /device:TPU:0 now
where the time goes in v1:
time: 115 us
  Pallas kernels  109 us (95%)
  local copies, waits for them, and re-layouts  2.93 us (3%)
  other arithmetic  1.3 us (1%)
  between operations  1.29 us (1%)
    pallas_call x1, Pallas kernels, step(): pl.pallas_call(functools.partial(body, odd, ring, rungs), out_shape=[jax....  109 us
    unnamed x3, local copies, waits for them, and re-layouts  2.93 us

profile of v1, /device:TPU:0, one launch (start us, length us, event | category | flops | bytes accessed | tf_op | source)
XLA Modules:
  0.0 114.7 jit_solution(6668903639999994380)
XLA Ops:
  0.6 1.3 %and_reduce_fusion = pred[]{:T(512)} fusion(s32[8]{0:T(128)} %param.9), kind=kLoop, calls=%fused_computation | loop fusion | flops 87 | bytes 33 | tf_op jit(solution)/shard_map/reduce_or | solution.py:344
  2.6 109.2 %conditional.1 = ((f32[1,6,96,768]{3,2,1,0:T(8,128)S(1)}, f32[1,6,96,768]{3,2,1,0:T(8,128)S(1)}, f32[1,5]{1,0:T(1,128)S(1)})) conditional(s32[]{:T(128)} %convert_element_type.3, (f32[8]{0:T(128)}, s32[8]{0:T(128)}, f32[1,6,96,768]{3,2,1,0:T(8,128)}, f32[1,6,96,768]{3,2,1,0:T(8,128)}) %tuple.13, (f32[8]{0:T(128)}, s32[8]{0:T(128)}, ...), branch_computations={%region_1.2_spmd, %region_2.3_spmd} | conditional | flops 66355200 | bytes 7077896 | solution.py:346
  2.6 109.2 %even_pairs.1 = (f32[1,6,96,768]{3,2,1,0:T(8,128)S(1)}, f32[1,6,96,768]{3,2,1,0:T(8,128)S(1)}, f32[1,5]{1,0:T(1,128)S(1)}) custom-call(f32[8]{0:T(128)} %get-tuple-element.42.kappas, s32[8]{0:T(128)} %get-tuple-element.17.partner, f32[1,6,96,768]{3,2,1,0:T(8,128)} %get-tuple-element.44.field, f32[1,6,96,768]{3,2,1,0:T(8,128)} %get-tuple-element.46.momenta), custom_call_target="tpu_custom_call" | custom-call | flops 66355200 | bytes 7077888 | tf_op jit(solution)/shard_map/cond/branch_0_fun/even_pairs/pallas_call | solution.py:304
  111.8 1.2 %copy.28 = f32[1,6,96,768]{3,2,1,0:T(8,128)} copy(f32[1,6,96,768]{3,2,1,0:T(8,128)S(1)} %get-tuple-element.57) | data formatting | bytes 3538944
  113.0 1.2 %copy.29 = f32[1,6,96,768]{3,2,1,0:T(8,128)} copy(f32[1,6,96,768]{3,2,1,0:T(8,128)S(1)} %get-tuple-element.58) | data formatting | bytes 3538944
  114.2 0.5 copy.30

commit v2 on v1

--- a/solution.py
+++ b/solution.py
@@ -12,7 +12,7 @@
 LAMBDA = 0.5
 STEP = 0.1
 
-ROWS = 16
+ROWS = 8
 LAG = 2
 STAGES = LEAPS + 1
 LANES = 128
@@ -118,12 +118,12 @@
             device_id=(mate, me), device_id_type=MESH,
         )
 
-    def first_halo(c, carry):
+    def first_halo(c):
         for copy in halo_copies(0, c):
             copy.start()
-        return carry
-
-    lax.fori_loop(0, chunks, first_halo, 0)
+
+    wedge = LAG * LEAPS - 1
+    lax.fori_loop(0, wedge, lambda c, carry: (first_halo(c), carry)[1], 0)
 
     acc[...] = jnp.zeros_like(acc)
     kappa = kappas[rung]
@@ -180,7 +180,16 @@
         if stage >= LEAPS - 1:
             when_paired(lambda: swap_copy(stage - LEAPS + 1, c).start())
 
+    for stage in range(LEAPS):
+        if stage == LEAPS // 2:
+            for c in range(wedge, min(wedge + LAG, chunks)):
+                first_halo(c)
+        lax.fori_loop(
+            0, wedge - LAG * stage, lambda k, carry, stage=stage: (unit(stage, stage + k), carry)[1], 0
+        )
+
     def iteration(i, carry):
+        pl.when(i + LAG < chunks)(lambda: first_halo(i + LAG))
         for stage in range(STAGES):
             k = i - LAG * stage
 
@@ -190,7 +199,7 @@
 
         return carry
 
-    lax.fori_loop(0, chunks + LAG * LEAPS, iteration, 0)
+    lax.fori_loop(wedge, chunks + LAG * LEAPS, iteration, 0)
 
     volume = float(planes * ring * height * width)
     for j in range(6):

time: 115 us -> 108 us (0.939)
  Pallas kernels: 109 us -> 102 us
    pallas_call x1, Pallas kernels: 109 us -> 102 us  [step(): pl.pallas_call(functools.partial(body, odd, ring, rungs), out_shape=[jax....]
where the time goes in v2:
time: 108 us
  Pallas kernels  102 us (94%)
  local copies, waits for them, and re-layouts  2.93 us (3%)
  other arithmetic  1.3 us (1%)
  between operations  1.29 us (1%)
    pallas_call x1, Pallas kernels, step(): pl.pallas_call(functools.partial(body, odd, ring, rungs), out_shape=[jax....  102 us
    unnamed x3, local copies, waits for them, and re-layouts  2.93 us

profile of v2, /device:TPU:0, one launch (start us, length us, event | category | flops | bytes accessed | tf_op | source)
XLA Modules:
  0.0 107.9 jit_solution(9946441416562423938)
XLA Ops:
  0.6 1.3 %and_reduce_fusion = pred[]{:T(512)} fusion(s32[8]{0:T(128)} %param.9), kind=kLoop, calls=%fused_computation | loop fusion | flops 87 | bytes 33 | tf_op jit(solution)/shard_map/reduce_or | solution.py:353
  2.6 102.4 %conditional.1 = ((f32[1,6,96,768]{3,2,1,0:T(8,128)S(1)}, f32[1,6,96,768]{3,2,1,0:T(8,128)S(1)}, f32[1,5]{1,0:T(1,128)S(1)})) conditional(s32[]{:T(128)} %convert_element_type.3, (f32[8]{0:T(128)}, s32[8]{0:T(128)}, f32[1,6,96,768]{3,2,1,0:T(8,128)}, f32[1,6,96,768]{3,2,1,0:T(8,128)}) %tuple.13, (f32[8]{0:T(128)}, s32[8]{0:T(128)}, ...), branch_computations={%region_1.2_spmd, %region_2.3_spmd} | conditional | flops 66355200 | bytes 7077896 | solution.py:355
  2.6 102.4 %even_pairs.1 = (f32[1,6,96,768]{3,2,1,0:T(8,128)S(1)}, f32[1,6,96,768]{3,2,1,0:T(8,128)S(1)}, f32[1,5]{1,0:T(1,128)S(1)}) custom-call(f32[8]{0:T(128)} %get-tuple-element.42.kappas, s32[8]{0:T(128)} %get-tuple-element.17.partner, f32[1,6,96,768]{3,2,1,0:T(8,128)} %get-tuple-element.44.field, f32[1,6,96,768]{3,2,1,0:T(8,128)} %get-tuple-element.46.momenta), custom_call_target="tpu_custom_call" | custom-call | flops 66355200 | bytes 7077888 | tf_op jit(solution)/shard_map/cond/branch_0_fun/even_pairs/pallas_call | solution.py:313
  105.0 1.2 %copy.28 = f32[1,6,96,768]{3,2,1,0:T(8,128)} copy(f32[1,6,96,768]{3,2,1,0:T(8,128)S(1)} %get-tuple-element.57) | data formatting | bytes 3538944
  106.2 1.2 %copy.29 = f32[1,6,96,768]{3,2,1,0:T(8,128)} copy(f32[1,6,96,768]{3,2,1,0:T(8,128)S(1)} %get-tuple-element.58) | data formatting | bytes 3538944
  107.4 0.5 copy.30

commit v3 on v2

--- a/solution.py
+++ b/solution.py
@@ -261,12 +261,26 @@
             arrived()
         out_copy(which, c, got).start()
 
+    def written(which, k):
+        c = lax.rem(LEAPS - 1 + which + k, chunks)
+        out_copy(which, c, got_f if which == 0 else got_p).wait()
+
     def finish(k, carry):
         for which in range(2):
-            settle(which, lax.rem(LEAPS - 1 + which + k, chunks))
+            c = lax.rem(LEAPS - 1 + which + k, chunks)
+            settle(which, c)
+            when_paired(lambda which=which, c=c: swap_copy(which, c).wait_send())
+            pl.when(k > 0)(lambda which=which, k=k: written(which, k - 1))
         return carry
 
-    lax.fori_loop(0, chunks, finish, 0)
+    def close(c, carry):
+        for stage in range(STAGES):
+            for copy in halo_copies(stage, c):
+                copy.wait_send()
+        return carry
+
+    lax.fori_loop(0, chunks, close, 0)
+    lax.fori_loop(0, chunks - 2, finish, 0)
 
     for off in range(1, rungs):
         there = lax.rem(rung + off, rungs)
@@ -286,20 +300,13 @@
     line = jnp.where(spot == 4, cumulative, line)
     stats[...] = line[:, 0:5]
 
-    def close(c, carry):
-        for stage in range(STAGES):
-            for copy in halo_copies(stage, c):
-                copy.wait_send()
-        for which in range(2):
-            when_paired(lambda which=which: swap_copy(which, c).wait_send())
-            out_copy(which, c, got_f if which == 0 else got_p).wait()
-        return carry
-
-    lax.fori_loop(0, chunks, close, 0)
     for off in range(1, ring):
         gx_copy(me, lax.rem(me + off, ring)).wait_send()
     for off in range(1, rungs):
         rung_copy(rung, lax.rem(rung + off, rungs)).wait_send()
+    lax.fori_loop(chunks - 2, chunks, finish, 0)
+    for which in range(2):
+        written(which, chunks - 1)
 
 
 def step(odd, kappas, partner, field, momenta):

time: 108 us -> 108 us (level)
  no operation moved by 1% of the time
where the time goes in v3:
time: 108 us
  Pallas kernels  103 us (95%)
  local copies, waits for them, and re-layouts  2.93 us (3%)
  other arithmetic  1.3 us (1%)
  between operations  1.29 us (1%)
    pallas_call x1, Pallas kernels, step(): pl.pallas_call(functools.partial(body, odd, ring, rungs), out_shape=[jax....  103 us
    unnamed x3, local copies, waits for them, and re-layouts  2.93 us

profile of v3, /device:TPU:0, one launch (start us, length us, event | category | flops | bytes accessed | tf_op | source)
XLA Modules:
  0.0 108.2 jit_solution(15884091106882782359)
XLA Ops:
  0.6 1.3 %and_reduce_fusion = pred[]{:T(512)} fusion(s32[8]{0:T(128)} %param.9), kind=kLoop, calls=%fused_computation | loop fusion | flops 87 | bytes 33 | tf_op jit(solution)/shard_map/reduce_or | solution.py:360
  2.6 102.7 %conditional.1 = ((f32[1,6,96,768]{3,2,1,0:T(8,128)S(1)}, f32[1,6,96,768]{3,2,1,0:T(8,128)S(1)}, f32[1,5]{1,0:T(1,128)S(1)})) conditional(s32[]{:T(128)} %convert_element_type.3, (f32[8]{0:T(128)}, s32[8]{0:T(128)}, f32[1,6,96,768]{3,2,1,0:T(8,128)}, f32[1,6,96,768]{3,2,1,0:T(8,128)}) %tuple.13, (f32[8]{0:T(128)}, s32[8]{0:T(128)}, ...), branch_computations={%region_1.2_spmd, %region_2.3_spmd} | conditional | flops 66355200 | bytes 7077896 | solution.py:362
  2.6 102.7 %odd_pairs.1 = (f32[1,6,96,768]{3,2,1,0:T(8,128)S(1)}, f32[1,6,96,768]{3,2,1,0:T(8,128)S(1)}, f32[1,5]{1,0:T(1,128)S(1)}) custom-call(f32[8]{0:T(128)} %get-tuple-element.43.kappas, s32[8]{0:T(128)} %get-tuple-element.21.partner, f32[1,6,96,768]{3,2,1,0:T(8,128)} %get-tuple-element.45.field, f32[1,6,96,768]{3,2,1,0:T(8,128)} %get-tuple-element.47.momenta), custom_call_target="tpu_custom_call" | custom-call | flops 66355200 | bytes 7077888 | tf_op jit(solution)/shard_map/cond/branch_1_fun/odd_pairs/pallas_call | solution.py:320
  105.3 1.2 %copy.28 = f32[1,6,96,768]{3,2,1,0:T(8,128)} copy(f32[1,6,96,768]{3,2,1,0:T(8,128)S(1)} %get-tuple-element.57) | data formatting | bytes 3538944
  106.5 1.2 %copy.29 = f32[1,6,96,768]{3,2,1,0:T(8,128)} copy(f32[1,6,96,768]{3,2,1,0:T(8,128)S(1)} %get-tuple-element.58) | data formatting | bytes 3538944
  107.7 0.5 copy.30
